TPU v7x, 32 devices: a whole 2x2x4 slice. The times are simulated.
32 devices in a mesh: groups: 2 (over y), tile: 16 (over z, x, core).
Axes of the slice: x: 2, y: 2, z: 4, core: 2. Of those that a mesh axis runs over, the one named last changes fastest.
Arguments:
- features: bfloat16 [192, 16, 16, 256], P(('groups', 'tile')), parts along dimension 0, may hold values from -6 to 6
- weights: bfloat16 [9, 256, 256], replicated, may hold values from -0.125 to 0.125
- grad_out: bfloat16 [192, 16, 16, 256], P(('groups', 'tile')), parts along dimension 0, may hold values from -6 to 6
- tile_pos: int32 [192], P(('groups', 'tile')), parts along dimension 0, may hold values from -1 to 7, as said below
- neighbours: int32 [192, 8], P(('groups', 'tile')), parts along dimension 0, may hold values from -1 to 15, as said below
Outputs:
- activation: bfloat16 [192, 16, 16, 256], P(('groups', 'tile')), parts along dimension 0
- weight_grad: float32 [18, 256, 256], P('groups'), parts along dimension 0
- input_grad: bfloat16 [192, 16, 16, 256], P(('groups', 'tile')), parts along dimension 0
There are 2 independent parts, one for each index of `groups`. A program takes and returns all parts, laid end to end along the dimension named above; an argument that names none is the same for every part. Nothing has to cross between parts.
Inputs may be any that keep to these rules, and one draw needn't show every extreme that they name: `tile_pos`: each device's 6 slots hold the tissue tiles of its band of 2 x 4 tiles first, in raster order, then empty slots; every device holds 2 or more tissue tiles and at least one device holds 6. A code c names slot c % 6 of the device whose index is the own index plus c // 6 - 1; codes of left and right neighbours name the own device, up and up-diagonal neighbours lie on the own or the preceding device, down and down-diagonal ones on the own or the following device. Neighbours are tissue tiles of the slide's grid and the relation is symmetric; empty slots and missing neighbours have -1.
All inputs are finite; a program needn't handle non-finite values.
Results may differ from a plain program's by a relative error of at most 0.0049.
Values may be sent and summed in bfloat16 or wider, within the bound.
A program may use at most 64 MiB of HBM per device.

v0:
```python
import math

import jax
import jax.numpy as jnp
from jax import lax
from jax.sharding import PartitionSpec as P

EDGE_PICK = (1, 0, 3, 2, 1, 1, 0, 0)
ROOT_HALF = 0.7071067811865476
INV_ROOT_TAU = 0.3989422804014327


def from_behind(value, axis, steps):
    count = lax.axis_size(axis)
    initial, last = (max(0, -steps), min(count, count - steps))
    return lax.ppermute(value, axis, [(source, source + steps) for source in range(initial, last)])


def gelu_value(preact):
    return preact * (0.5 * (1.0 + lax.erf(preact * ROOT_HALF)))


def gelu_slope(preact):
    cumulative = 0.5 * (1.0 + lax.erf(preact * ROOT_HALF))
    density = jnp.exp(-0.5 * preact * preact) * INV_ROOT_TAU
    return cumulative + preact * density


def edge_rims(field_map):
    return jnp.stack(
        [field_map[:, 0], field_map[:, -1], field_map[:, :, 0], field_map[:, :, -1]], axis=1
    )


def surround(center, gathered):
    upper_row = jnp.concatenate([gathered[:, 4, -1:], gathered[:, 0], gathered[:, 5, :1]], axis=1)
    lower_row = jnp.concatenate([gathered[:, 6, -1:], gathered[:, 1], gathered[:, 7, :1]], axis=1)
    middle = jnp.concatenate(
        [gathered[:, 2][:, :, None], center, gathered[:, 3][:, :, None]], axis=2
    )
    return jnp.concatenate([upper_row[:, None], middle, lower_row[:, None]], axis=1)


def tap_matrix(extended, flipped):
    side_cells = extended.shape[1] - 2
    pieces = []
    for row_tap in range(3):
        for col_tap in range(3):
            row_start = 2 - row_tap if flipped else row_tap
            col_start = 2 - col_tap if flipped else col_tap
            pieces.append(
                extended[:, row_start : row_start + side_cells, col_start : col_start + side_cells]
            )
    stacked = jnp.concatenate(pieces, axis=-1)
    return stacked.reshape(-1, stacked.shape[-1])


def lookup(edge_table, source, linked):
    clipped = jnp.clip(jnp.where(linked, source, 0), 0, edge_table.shape[0] - 1)
    picked = jnp.take(edge_table, clipped.reshape(-1), axis=0).reshape(
        linked.shape + edge_table.shape[1:]
    )
    return jnp.where(linked[:, :, None, None], picked, jnp.zeros((), picked.dtype))


def narrow_sources(neighbours, edge_picks, tile_dev):
    anchor = neighbours // tile_dev
    own_slot = (neighbours - tile_dev) * 4 + edge_picks[None, :]
    return jnp.where(
        anchor == 1,
        own_slot,
        jnp.where(anchor == 0, 4 * tile_dev + neighbours, 3 * tile_dev + neighbours),
    )


def narrow_table(own_rims, upper_rows, lower_rows):
    tile_dev = own_rims.shape[0]
    side_cells = own_rims.shape[2]
    channels = own_rims.shape[3]
    return jnp.concatenate(
        [own_rims.reshape(4 * tile_dev, side_cells, channels), upper_rows, lower_rows], axis=0
    )


def forward_tiles(extended, grad_tiles, tissue_gate, weight_mat):
    tile_count = extended.shape[0]
    side_cells = extended.shape[1] - 2
    channels = weight_mat.shape[1]
    preact = jnp.dot(tap_matrix(extended, False), weight_mat, preferred_element_type=jnp.float32)
    preact = preact.reshape(tile_count, side_cells, side_cells, channels)
    gate_cells = tissue_gate[:, None, None, None]
    act_map = (gelu_value(preact) * gate_cells).astype(jnp.bfloat16)
    slope_map = (grad_tiles.astype(jnp.float32) * gelu_slope(preact) * gate_cells).astype(
        jnp.bfloat16
    )
    return (act_map, slope_map)


def weight_terms(ext_x, slope_map):
    return lax.dot_general(
        tap_matrix(ext_x, False),
        slope_map.reshape(-1, slope_map.shape[-1]),
        (((0,), (0,)), ((), ())),
        preferred_element_type=jnp.float32,
    )


def backward_tiles(ext_g, tissue_gate, flip_mat):
    tile_count = ext_g.shape[0]
    side_cells = ext_g.shape[1] - 2
    channels = flip_mat.shape[1]
    back_map = jnp.dot(tap_matrix(ext_g, True), flip_mat, preferred_element_type=jnp.float32)
    back_map = (
        back_map.reshape(tile_count, side_cells, side_cells, channels)
        * tissue_gate[:, None, None, None]
    )
    return back_map.astype(jnp.bfloat16)


def body(features, weights, grad_out, tile_pos, neighbours):
    tile_dev = features.shape[0]
    side_cells = features.shape[1]
    channels = features.shape[3]
    devices = lax.axis_size("tile")
    tissue = (tile_pos >= 0).astype(jnp.float32)
    weight_mat = weights.reshape(9 * channels, channels)
    flip_mat = jnp.transpose(weights, (0, 2, 1)).reshape(9 * channels, channels)
    edge_picks = jnp.array(EDGE_PICK, dtype=jnp.int32)
    linked = neighbours >= 0
    rims_x = edge_rims(features)
    from_above = from_behind(rims_x[:, 1], "tile", 1)
    from_below = from_behind(rims_x[:, 0], "tile", -1)
    table_x = narrow_table(rims_x, from_above, from_below)
    source = narrow_sources(neighbours, edge_picks, tile_dev)
    ext_x = surround(features, lookup(table_x, source, linked))
    activation, pre_grad = forward_tiles(ext_x, grad_out, tissue, weight_mat)
    rims_g = edge_rims(pre_grad)
    grad_above = from_behind(rims_g[:, 1], "tile", 1)
    grad_below = from_behind(rims_g[:, 0], "tile", -1)
    table_g = narrow_table(rims_g, grad_above, grad_below)
    ext_g = surround(pre_grad, lookup(table_g, source, linked))
    weight_part = weight_terms(ext_x, pre_grad)
    grad_scale = 1.0 / math.sqrt(tile_dev * devices * side_cells * side_cells)
    summed = lax.psum(weight_part, "tile")
    weight_grad = (summed * grad_scale).reshape(9, channels, channels)
    input_grad = backward_tiles(ext_g, tissue, flip_mat)
    return (activation, weight_grad, input_grad)


def solution(mesh):
    in_specs = (
        P(("groups", "tile"), None, None, None),
        P(),
        P(("groups", "tile"), None, None, None),
        P(("groups", "tile")),
        P(("groups", "tile"), None),
    )
    out_specs = (
        P(("groups", "tile"), None, None, None),
        P("groups", None, None),
        P(("groups", "tile"), None, None, None),
    )
    return jax.shard_map(body, mesh=mesh, in_specs=in_specs, out_specs=out_specs, check_vma=False)
```

profile of v0, /device:TPU:0, one launch (start us, length us, event | category | flops | bytes accessed | tf_op | source)
XLA Modules:
  0.0 143.1 jit_solution(6044019779046628402)
XLA Ops:
  7.2 0.9 slice_bitcast_fusion.11
  8.2 1.3 collective-permute-start.1
  9.5 3.0 %collective-permute-start = (bf16[6,16,256]{2,1,0:T(8,128)(2,1)S(1)}, bf16[6,16,256]{2,1,0:T(8,128)(2,1)S(1)}, u32[]{:S(2)}, u32[]{:S(2)}) collective-permute-start(bf16[6,16,256]{2,1,0:T(8,128)(2,1)S(1)} %get-tuple-element.18), channel_id=1, source_target_pairs={{0,1},{1,2},{2,3},{3,4},{4,5},{5,6},{6,7},{7,8},{8,9},{9,10},{10,1... | collective-permute-start | bytes 147464 | tf_op jit(solution)/shard_map/ppermute | solution.py:16
  12.5 1.3 fusion.14
  13.8 0.7 select_clamp_fusion
  14.6 0.7 broadcast_compare_fusion
  15.3 0.7 compare_convert_fusion
  16.1 1.6 %copy.89 = bf16[9,256,256]{1,2,0:T(8,128)(2,1)} copy(bf16[9,256,256]{2,1,0:T(8,128)(2,1)S(1)} %copy-done.1) | data formatting | bytes 2359296 | tf_op args[1]
  17.8 0.6 gather_fusion
  18.9 1.2 pad_maximum_fusion
  20.6 0.3 slice_dynamic-update-slice_fusion.9
  20.9 0.4 fusion.10
  21.3 0.5 fusion.9
  21.9 0.3 slice_dynamic-update-slice_fusion.7
  22.2 0.3 slice_dynamic-update-slice_fusion.6
  22.5 0.4 copy-done.3
  22.9 3.6 %fusion.6 = (bf16[6,16,16,256]{3,2,1,0:T(8,128)(2,1)S(1)}, bf16[6,16,16,256]{3,2,1,0:T(8,128)(2,1)}) fusion(bf16[6,16,16,256]{3,2,1,0:T(8,128)(2,1)S(1)} %copy-done.3, f32[6]{0:T(128)S(1)} %compare_convert_fusion, bf16[6,16,16,2304]{3,2,1,0:T(8,128)(2,1)S(1)} %slice_dynamic-update-slice_fusion.6, bf16[2304,256,1,1]{1,0,3,2:T(8,128)(2,1)S(1)} %bitcast.104), kind=kOutput, calls=%fused_computation.10 | convolution fusion | flops 1817837568 | bytes 10616856 | tf_op jit(solution)/shard_map/dot_general | solution.py:89
  26.5 3.5 %convolution_bitcast_fusion = f32[2304,256]{1,0:T(8,128)} fusion(bf16[6,16,16,2304]{3,2,1,0:T(8,128)(2,1)S(1)} %slice_dynamic-update-slice_fusion.6, bf16[6,16,16,256]{3,2,1,0:T(8,128)(2,1)S(1)} %get-tuple-element.4), kind=kOutput, calls=%fused_computation.2 | convolution fusion | flops 1811939328 | bytes 10223616 | tf_op jit(solution)/shard_map/dot_general | solution.py:100
  30.2 1.3 collective-permute-start.3
  31.5 5.3 %collective-permute-start.2 = (bf16[6,16,256]{2,1,0:T(8,128)(2,1)S(1)}, bf16[6,16,256]{2,1,0:T(8,128)(2,1)S(1)}, u32[]{:S(2)}, u32[]{:S(2)}) collective-permute-start(bf16[6,16,256]{2,1,0:T(8,128)(2,1)S(1)} %get-tuple-element.12), channel_id=1, source_target_pairs={{0,1},{1,2},{2,3},{3,4},{4,5},{5,6},{6,7},{7,8},{8,9},{9,10},{10,1... | collective-permute-start | bytes 147464 | tf_op jit(solution)/shard_map/ppermute | solution.py:16
  36.9 0.6 collective-permute-done.2
  37.5 0.6 gather_fusion.1
  38.7 1.2 maximum_maximum_fusion.1
  40.2 0.3 slice_dynamic-update-slice_fusion.4
  40.6 0.5 fusion.8
  41.1 0.4 fusion.7
  41.5 0.3 slice_dynamic-update-slice_fusion.2
  41.8 0.3 slice_dynamic-update-slice_fusion.1
  42.2 0.5 copy-done.2
  42.7 3.0 %multiply_convert_fusion = bf16[6,16,16,256]{3,2,1,0:T(8,128)(2,1)} fusion(bf16[6,16,16,2304]{3,2,1,0:T(8,128)(2,1)S(1)} %slice_dynamic-update-slice_fusion, bf16[2304,256,1,1]{1,0,3,2:T(8,128)(2,1)S(1)} %bitcast.105, f32[6]{0:T(128)S(1)} %compare_convert_fusion), kind=kOutput, calls=%fused_computation.11 | convolution fusion | flops 1812725760 | bytes 9043992 | tf_op jit(solution)/shard_map/dot_general | solution.py:112
  45.7 87.3 %all-reduce.2.cloned.1.call-done = f32[2304,256]{1,0:T(8,128)} async-done(((f32[2304,256]{1,0:T(8,128)}), f32[2304,256]{1,0:T(8,128)}) %all-reduce.2.cloned.1.call-update) | async-done | bytes 2359312 | tf_op jit(solution)/shard_map/psum | solution.py:144
  133.0 3.3 %broadcast_multiply_fusion = f32[2304,256]{1,0:T(8,128)} fusion(f32[2304,256]{1,0:T(8,128)} %all-reduce.2.cloned.1.call-done), kind=kLoop, calls=%fused_computation.18 | loop fusion | flops 589824 | bytes 4718592 | tf_op jit(solution)/shard_map/mul | solution.py:145
  (50 shorter events, 2.6 us)
Async XLA Ops:
  7.2 9.0 %copy-start.1 = (bf16[9,256,256]{2,1,0:T(8,128)(2,1)S(1)}, bf16[9,256,256]{2,1,0:T(8,128)(2,1)}, u32[]{:S(2)}) copy-start(bf16[9,256,256]{2,1,0:T(8,128)(2,1)} %param.9) | copy-start | bytes 3538948
  7.2 125.8 %all-reduce.2.cloned.1.call-start = ((), (), s32[]{:S(2)}) async-start(), calls=%async_computation | async-start | bytes 4718592 | tf_op jit(solution)/shard_map/psum | solution.py:144
  8.2 9.6 %collective-permute-start.1 = (bf16[6,16,256]{2,1,0:T(8,128)(2,1)S(1)}, bf16[6,16,256]{2,1,0:T(8,128)(2,1)S(1)}, u32[]{:S(2)}, u32[]{:S(2)}) collective-permute-start(bf16[6,16,256]{2,1,0:T(8,128)(2,1)S(1)} %get-tuple-element.17), channel_id=1, source_target_pairs={{1,0},{2,1},{3,2},{4,3},{5,4},{6,5},{7,6},{8,7},{9,8},{10,9},{11,1... | collective-permute-start | bytes 147464 | tf_op jit(solution)/shard_map/ppermute | solution.py:16
  9.5 8.3 %collective-permute-start = (bf16[6,16,256]{2,1,0:T(8,128)(2,1)S(1)}, bf16[6,16,256]{2,1,0:T(8,128)(2,1)S(1)}, u32[]{:S(2)}, u32[]{:S(2)}) collective-permute-start(bf16[6,16,256]{2,1,0:T(8,128)(2,1)S(1)} %get-tuple-element.18), channel_id=1, source_target_pairs={{0,1},{1,2},{2,3},{3,4},{4,5},{5,6},{6,7},{7,8},{8,9},{9,10},{10,1... | collective-permute-start | bytes 147464 | tf_op jit(solution)/shard_map/ppermute | solution.py:16
  17.7 1.2 copy-start
  21.8 1.1 copy-start.3
  30.2 6.7 %collective-permute-start.3 = (bf16[6,16,256]{2,1,0:T(8,128)(2,1)S(1)}, bf16[6,16,256]{2,1,0:T(8,128)(2,1)S(1)}, u32[]{:S(2)}, u32[]{:S(2)}) collective-permute-start(bf16[6,16,256]{2,1,0:T(8,128)(2,1)S(1)} %get-tuple-element.11), channel_id=1, source_target_pairs={{1,0},{2,1},{3,2},{4,3},{5,4},{6,5},{7,6},{8,7},{9,8},{10,9},{11,1... | collective-permute-start | bytes 147464 | tf_op jit(solution)/shard_map/ppermute | solution.py:16
  31.5 6.0 %collective-permute-start.2 = (bf16[6,16,256]{2,1,0:T(8,128)(2,1)S(1)}, bf16[6,16,256]{2,1,0:T(8,128)(2,1)S(1)}, u32[]{:S(2)}, u32[]{:S(2)}) collective-permute-start(bf16[6,16,256]{2,1,0:T(8,128)(2,1)S(1)} %get-tuple-element.12), channel_id=1, source_target_pairs={{0,1},{1,2},{2,3},{3,4},{4,5},{5,6},{6,7},{7,8},{8,9},{9,10},{10,1... | collective-permute-start | bytes 147464 | tf_op jit(solution)/shard_map/ppermute | solution.py:16
  41.5 1.3 copy-start.2
Sparse Core Ops, SparseCore 0:
  30.4 102.5 all-reduce.1
where the time goes:
time: 144 us; the launch traced here: 143 us
  waiting for transfers between devices  87.9 us (61%)
  between operations  14.4 us (10%)
  starting transfers between devices  10.9 us (8%)
  other arithmetic  10.2 us (7%)
  matrix products  10 us (7%)
  local copies, waits for them, and re-layouts  9.6 us (7%)
    psum x1, waiting for transfers between devices, body(): summed = lax.psum(weight_part, 'tile')  87.3 us
    ppermute x4, starting transfers between devices, from_behind(): lax.ppermute(value, axis, [(source, source + steps) for source in range(i...  10.9 us
    unnamed x24, local copies, waits for them, and re-layouts  5.97 us
    dot_general x1, matrix products, forward_tiles(): jnp.dot(tap_matrix(extended, False), weight_mat, preferred_element_type=j...  3.56 us
    dot_general x1, matrix products, weight_terms(): lax.dot_general(tap_matrix(ext_x, False), slope_map.reshape(-1, slope_map...  3.52 us
    mul x1, other arithmetic, body(): weight_grad = (summed * grad_scale).reshape(9, channels, channels)  3.27 us
    dot_general x1, matrix products, backward_tiles(): jnp.dot(tap_matrix(ext_g, True), flip_mat, preferred_element_type=jnp.flo...  2.96 us
  transfers between devices with their start and end apart: 5, of which 2 were waited for; matrix products, arithmetic and copies ran while one was open for 9% of the time, Pallas kernels for 0%

commit v1 on v0

v1 whole, which is shorter than its diff:
```python
import functools
import math

import jax
import jax.numpy as jnp
from jax import lax
from jax.experimental import pallas as pl
from jax.experimental.pallas import tpu as pltpu
from jax.sharding import PartitionSpec as P

ROOT_HALF = 0.7071067811865476
INV_ROOT_TAU = 0.3989422804014327
FAN = 4
LAG_CORE, LAG_NEAR, LAG_FAN, LAG_FAN_BACK, LAG_NEAR_BACK, LAG_CORE_BACK = (1, 3, 5, 7, 9, 10)
MESH = pl.DeviceIdType.MESH


def shifted(center, left, right, axis):
    cell = lax.broadcasted_iota(jnp.int32, center.shape, axis)
    side = center.shape[axis]
    from_left = pltpu.roll(jnp.where(cell == side - 1, left, center), 1, axis)
    from_right = pltpu.roll(jnp.where(cell == 0, right, center), side - 1, axis)
    return from_left, from_right


def kernel(
    count,
    scale,
    features,
    weights,
    grad_out,
    tile_pos,
    links,
    act,
    grad_sum,
    input_grad,
    ext_x,
    ext_g,
    above_x,
    below_x,
    above_g,
    below_g,
    rows_out,
    pre_grad,
    pre_grad_t,
    weights_t,
    part,
    core_out,
    core_in,
    near_out,
    near_in,
    fan_out,
    fan_in,
    far_out,
    far_in,
    total,
    halo_sems,
    core_sems,
    near_sems,
    fan_sems,
    far_sems,
):
    f32, bf16 = jnp.float32, jnp.bfloat16
    tiles, side, _, channels = features.shape
    cells = side * side
    taps = weights.shape[0]
    zero_row = 2 * tiles
    me = lax.axis_index("tile")
    core = lax.rem(me, 2)
    near = lax.rem(me // 2, 2)
    fan = lax.rem(me // 4, FAN)
    base = me - core - 2 * near - 4 * fan
    core_peer = me + 1 - 2 * core
    near_peer = me + 2 - 4 * near
    far_rounds = far_out.shape[1]

    def fan_slot(step):
        return lax.rem(fan + step + FAN, FAN)

    def fan_peer(step):
        return base + 4 * fan_slot(step) + 2 * near + core

    def far_peer(turn):
        stride = 4 * FAN * 2**turn
        return me + stride - 2 * stride * lax.rem(me // stride, 2)

    def send(source, target, sems, peer):
        return pltpu.make_async_remote_copy(
            src_ref=source,
            dst_ref=target,
            send_sem=sems.at[0],
            recv_sem=sems.at[1],
            device_id={"tile": peer},
            device_id_type=MESH,
        )

    has_prev, has_next = me > 0, me < count - 1
    barrier = pltpu.get_barrier_semaphore()
    peers = [core_peer, near_peer] + [fan_peer(step) for step in range(1, FAN)]
    peers = peers + [far_peer(turn) for turn in range(far_rounds)]
    for peer in peers:
        pl.semaphore_signal(barrier, inc=1, device_id={"tile": peer}, device_id_type=MESH)

    @pl.when(has_prev)
    def _():
        pl.semaphore_signal(barrier, inc=1, device_id={"tile": me - 1}, device_id_type=MESH)

    @pl.when(has_next)
    def _():
        pl.semaphore_signal(barrier, inc=1, device_id={"tile": me + 1}, device_id_type=MESH)

    pl.semaphore_wait(barrier, len(peers) + jnp.where(has_prev, 1, 0) + jnp.where(has_next, 1, 0))

    def halo(turn, above, below):
        down = send(rows_out.at[turn, 0], above.at[pl.ds(0, tiles)], halo_sems.at[turn, 0], me + 1)
        up = send(rows_out.at[turn, 1], below.at[pl.ds(tiles, tiles)], halo_sems.at[turn, 1], me - 1)
        return down, up

    def start_halo(turn, field, above, below):
        last, first = field[:, side - 1], field[:, 0]
        rows_out[turn, 0] = last
        rows_out[turn, 1] = first
        down, up = halo(turn, above, below)

        @pl.when(has_next)
        def _():
            down.start()

        @pl.when(has_prev)
        def _():
            up.start()

        above[tiles : 2 * tiles] = last
        below[0:tiles] = first
        for table in (above, below):
            table[zero_row] = jnp.zeros(table.shape[1:], table.dtype)

    def wait_halo(turn, above, below):
        down, up = halo(turn, above, below)

        @pl.when(has_next)
        def _():
            down.wait_send()
            up.wait_recv()

        @pl.when(has_prev)
        def _():
            up.wait_send()
            down.wait_recv()

    def link_gate(code):
        return jnp.where(code >= 0, 1.0, 0.0).astype(f32)

    def inner_rows(field, tile, put):
        center = field[tile]
        left, right = links[tile, 2], links[tile, 3]
        left_map = field[jnp.where(left >= tiles, left - tiles, tile)].astype(f32) * link_gate(left)
        right_map = field[jnp.where(right >= tiles, right - tiles, tile)].astype(f32) * link_gate(right)
        from_left, from_right = shifted(center.astype(f32), left_map, right_map, 1)
        inner = slice(1, side + 1)
        put(0, inner, from_left.astype(bf16))
        put(1, inner, center)
        put(2, inner, from_right.astype(bf16))

    def border_rows(table, row, tile, first_link, left_link, right_link, base_code, put):
        def pick(link):
            code = links[tile, link]
            return table[jnp.where(code >= base_code, code - base_code, zero_row)]

        center = pick(first_link)
        from_left, from_right = shifted(
            center.astype(f32), pick(left_link).astype(f32), pick(right_link).astype(f32), 0
        )
        put(0, row, from_left.astype(bf16))
        put(1, row, center)
        put(2, row, from_right.astype(bf16))

    def both_borders(above, below, tile, put):
        border_rows(above, 0, tile, 0, 4, 5, 0, put)
        border_rows(below, side + 1, tile, 1, 6, 7, tiles, put)

    start_halo(0, features, above_x, below_x)

    def put_x(tile):
        def put(shift, rows, value):
            ext_x[shift, tile, rows] = value

        return put

    @pl.loop(0, tiles)
    def _(tile):
        inner_rows(features, tile, put_x(tile))

    wait_halo(0, above_x, below_x)

    @pl.loop(0, tiles)
    def _(tile):
        both_borders(above_x, below_x, tile, put_x(tile))

    weight_mat_rows = taps * channels

    @pl.loop(0, tiles)
    def _(tile):
        pieces = [
            ext_x[b, tile, a : a + side].reshape(cells, channels) for a in range(3) for b in range(3)
        ]
        preact = jnp.dot(
            jnp.concatenate(pieces, axis=1),
            weights[...].reshape(weight_mat_rows, channels),
            preferred_element_type=f32,
        )
        gate = jnp.where(tile_pos[tile] >= 0, 1.0, 0.0).astype(f32)
        cumulative = 0.5 * (1.0 + lax.erf(preact * ROOT_HALF))
        density = jnp.exp(-0.5 * preact * preact) * INV_ROOT_TAU
        act[tile] = (preact * cumulative * gate).astype(bf16).reshape(side, side, channels)
        grad = grad_out[tile].reshape(cells, channels).astype(f32)
        slope = grad * (cumulative + preact * density) * gate
        pre_grad[tile] = slope.astype(bf16).reshape(side, side, channels)
        pre_grad_t[tile] = slope.T.astype(bf16)

    start_halo(1, pre_grad, above_g, below_g)

    def core_copy(k):
        return send(core_out.at[k], core_in.at[k], core_sems.at[0, k], core_peer)

    def near_copy(k):
        return send(near_out.at[k], near_in.at[k], near_sems.at[0, k], near_peer)

    def fan_copy(k, step):
        return send(
            fan_out.at[k, step - 1],
            fan_in.at[k, step - 1],
            fan_sems.at[0, k, step - 1],
            fan_peer(step),
        )

    def far_copy(k, turn):
        return send(far_out.at[k, turn], far_in.at[k, turn], far_sems.at[k, turn], far_peer(turn))

    def fan_back(k, step, owner):
        block = total.at[k, core, near, owner]
        return send(block, block, fan_sems.at[1, k, step - 1], fan_peer(step))

    def near_back(k, owner):
        block = total.at[k, core, owner]
        return send(block, block, near_sems.at[1, k], near_peer)

    def core_back(k, owner):
        block = total.at[k, owner]
        return send(block, block, core_sems.at[1, k], core_peer)

    @pl.loop(0, taps + LAG_CORE_BACK)
    def _(step):
        @pl.when(step < taps)
        def _():
            k = step
            rows = ext_x[lax.rem(k, 3), :, pl.ds(k // 3, side)].reshape(tiles * cells, channels)
            lhs = jnp.concatenate([pre_grad_t[tile] for tile in range(tiles)], axis=1)
            term = jnp.dot(lhs, rows, preferred_element_type=f32)
            part[k] = term.T.reshape(part.shape[1:])
            core_out[k] = part[k, 1 - core].astype(bf16)
            core_copy(k).start()
            weights_t[k] = weights[k].astype(f32).T.astype(bf16)

        @pl.when((step >= LAG_CORE) & (step < taps + LAG_CORE))
        def _():
            k = step - LAG_CORE
            core_copy(k).wait_recv()
            part[k, core] = part[k, core] + core_in[k].astype(f32)
            near_out[k] = part[k, core, 1 - near].astype(bf16)
            near_copy(k).start()

        @pl.when((step >= LAG_NEAR) & (step < taps + LAG_NEAR))
        def _():
            k = step - LAG_NEAR
            near_copy(k).wait_recv()
            part[k, core, near] = part[k, core, near] + near_in[k].astype(f32)
            for turn in range(1, FAN):
                fan_out[k, turn - 1] = part[k, core, near, fan_slot(turn)].astype(bf16)
                fan_copy(k, turn).start()

        @pl.when((step >= LAG_FAN) & (step < taps + LAG_FAN))
        def _():
            k = step - LAG_FAN
            sums = part[k, core, near, fan]
            for turn in range(1, FAN):
                fan_copy(k, turn).wait_recv()
                sums = sums + fan_in[k, turn - 1].astype(f32)
            for turn in range(far_rounds):
                far_out[k, turn] = sums.astype(bf16)
                copy = far_copy(k, turn)
                copy.start()
                copy.wait()
                sums = far_out[k, turn].astype(f32) + far_in[k, turn].astype(f32)
            total[k, core, near, fan] = (sums * scale).astype(bf16)
            for turn in range(1, FAN):
                fan_back(k, turn, fan).start()

        @pl.when((step >= LAG_FAN_BACK) & (step < taps + LAG_FAN_BACK))
        def _():
            k = step - LAG_FAN_BACK
            for turn in range(1, FAN):
                fan_back(k, turn, fan_slot(-turn)).wait_recv()
            near_back(k, near).start()

        @pl.when((step >= LAG_NEAR_BACK) & (step < taps + LAG_NEAR_BACK))
        def _():
            k = step - LAG_NEAR_BACK
            near_back(k, 1 - near).wait_recv()
            core_back(k, core).start()

        @pl.when(step >= LAG_CORE_BACK)
        def _():
            k = step - LAG_CORE_BACK
            core_back(k, 1 - core).wait_recv()
            core_copy(k).wait_send()
            near_copy(k).wait_send()
            for turn in range(1, FAN):
                fan_copy(k, turn).wait_send()
                fan_back(k, turn, fan).wait_send()
            near_back(k, near).wait_send()
            core_back(k, core).wait_send()
            grad_sum[k] = total[k].reshape(channels, channels)

        @pl.when(step == taps)
        def _():
            wait_halo(1, above_g, below_g)

        @pl.when((step >= taps) & (step < taps + tiles))
        def _():
            tile = step - taps

            def put(shift, rows, value):
                ext_g[shift, rows] = value

            inner_rows(pre_grad, tile, put)
            both_borders(above_g, below_g, tile, put)
            pieces = [
                ext_g[2 - b, 2 - a : 2 - a + side].reshape(cells, channels)
                for a in range(3)
                for b in range(3)
            ]
            back = jnp.dot(
                jnp.concatenate(pieces, axis=1),
                weights_t[...].reshape(weight_mat_rows, channels),
                preferred_element_type=f32,
            )
            gate = jnp.where(tile_pos[tile] >= 0, 1.0, 0.0).astype(f32)
            input_grad[tile] = (back * gate).astype(bf16).reshape(side, side, channels)


def body(count, features, weights, grad_out, tile_pos, neighbours):
    bf16, f32 = jnp.bfloat16, jnp.float32
    tiles, side, _, channels = features.shape
    taps = weights.shape[0]
    scale = 1.0 / math.sqrt(tiles * count * side * side)
    split = (2, 2, FAN, channels // (4 * FAN), channels)
    far_rounds = int(math.log2(count // (4 * FAN)))
    table = pltpu.VMEM((2 * tiles + 1, side, channels), bf16)
    dma = pltpu.SemaphoreType.DMA
    vmem = pl.BlockSpec(memory_space=pltpu.VMEM)
    smem = pl.BlockSpec(memory_space=pltpu.SMEM)
    flops = 3 * 2 * tiles * side * side * taps * channels * channels
    act, grad_sum, input_grad = pl.pallas_call(
        functools.partial(kernel, count, scale),
        out_shape=(
            jax.ShapeDtypeStruct(features.shape, bf16),
            jax.ShapeDtypeStruct(weights.shape, bf16),
            jax.ShapeDtypeStruct(features.shape, bf16),
        ),
        in_specs=[vmem, vmem, vmem, smem, smem],
        out_specs=(vmem, vmem, vmem),
        scratch_shapes=[
            pltpu.VMEM((3, tiles, side + 2, side, channels), bf16),
            pltpu.VMEM((3, side + 2, side, channels), bf16),
            table,
            table,
            table,
            table,
            pltpu.VMEM((2, 2, tiles, side, channels), bf16),
            pltpu.VMEM(features.shape, bf16),
            pltpu.VMEM((tiles, channels, side * side), bf16),
            pltpu.VMEM(weights.shape, bf16),
            pltpu.VMEM((taps,) + split, f32),
            pltpu.VMEM((taps,) + split[1:], bf16),
            pltpu.VMEM((taps,) + split[1:], bf16),
            pltpu.VMEM((taps,) + split[2:], bf16),
            pltpu.VMEM((taps,) + split[2:], bf16),
            pltpu.VMEM((taps, FAN - 1) + split[3:], bf16),
            pltpu.VMEM((taps, FAN - 1) + split[3:], bf16),
            pltpu.VMEM((taps, far_rounds) + split[3:], bf16),
            pltpu.VMEM((taps, far_rounds) + split[3:], bf16),
            pltpu.VMEM((taps,) + split, bf16),
            dma((2, 2, 2)),
            dma((2, taps, 2)),
            dma((2, taps, 2)),
            dma((2, taps, FAN - 1, 2)),
            dma((taps, far_rounds, 2)),
        ],
        compiler_params=pltpu.CompilerParams(
            collective_id=0, has_side_effects=True, vmem_limit_bytes=48 * 2**20
        ),
        cost_estimate=pl.CostEstimate(flops=flops, bytes_accessed=2**23, transcendentals=0),
        name="tile_conv_step",
    )(features, weights, grad_out, tile_pos, neighbours)
    return act, grad_sum.astype(f32), input_grad


def solution(mesh):
    in_specs = (
        P(("groups", "tile"), None, None, None),
        P(),
        P(("groups", "tile"), None, None, None),
        P(("groups", "tile")),
        P(("groups", "tile"), None),
    )
    out_specs = (
        P(("groups", "tile"), None, None, None),
        P("groups", None, None),
        P(("groups", "tile"), None, None, None),
    )
    return jax.shard_map(
        functools.partial(body, mesh.shape["tile"]),
        mesh=mesh,
        in_specs=in_specs,
        out_specs=out_specs,
        check_vma=False,
    )
```

time: 144 us -> 51.2 us (0.36)
  waiting for transfers between devices: 87.9 us -> 0 us
  Pallas kernels: 0 us -> 42 us
  between operations: 14.4 us -> 0.65 us
  starting transfers between devices: 10.9 us -> 0 us
  matrix products: 10 us -> 0 us
  other arithmetic: 10.2 us -> 1.63 us
  local copies, waits for them, and re-layouts: 9.6 us -> 6.63 us
    psum x1 -> x0, waiting for transfers between devices: 87.3 us -> none  [body(): summed = lax.psum(weight_part, 'tile')]
    pallas_call x0 -> x1, Pallas kernels: none -> 42 us  [body(): pl.pallas_call(functools.partial(kernel, count, scale), out_shape=(jax.Sh...]
    ppermute x4 -> x0, starting transfers between devices: 10.9 us -> none  [from_behind(): lax.ppermute(value, axis, [(source, source + steps) for source in range(i...]
    dot_general x3 -> x0, matrix products: 10 us -> none  [the longest x1 3.56 us: forward_tiles(): jnp.dot(tap_matrix(extended, False), weight_mat, preferred_element_type=j...]
    mul x1 -> x0, other arithmetic: 3.27 us -> none  [body(): weight_grad = (summed * grad_scale).reshape(9, channels, channels)]
    concatenate x4 -> x0, other arithmetic: 2.5 us -> none  [the longest x2 2.42 us: surround(): jnp.concatenate([upper_row[:, None], middle, lower_row[:, None]], axis=1)]
    unnamed x4 -> x0, other arithmetic: 1.67 us -> none
    slice x3 -> x0, local copies, waits for them, and re-layouts: 1.48 us -> none  [the longest x2 1.47 us: edge_rims(): field_map[:, :, 0]]
  transfers between devices with their start and end apart: 5 -> 0, of which waited for: 2 -> 0; matrix products, arithmetic and copies ran while one was open for 9% -> 0% of each run, Pallas kernels for 0% -> 0%
where the time goes in v1:
time: 51.2 us; the launch traced here: 50.9 us
  Pallas kernels  42 us (82%)
  local copies, waits for them, and re-layouts  6.63 us (13%)
  other arithmetic  1.63 us (3%)
  between operations  0.65 us (1%)
    pallas_call x1, Pallas kernels, body(): pl.pallas_call(functools.partial(kernel, count, scale), out_shape=(jax.Sh...  42 us
    unnamed x12, local copies, waits for them, and re-layouts  6.63 us
    convert_element_type x1, other arithmetic, body(): return (act, grad_sum.astype(f32), input_grad)  1.63 us

profile of v1, /device:TPU:0, one launch (start us, length us, event | category | flops | bytes accessed | tf_op | source)
XLA Modules:
  0.0 50.9 jit_solution(7839942274437195574)
XLA Ops:
  0.6 0.0 copy-start
  0.6 1.3 %copy-done = bf16[9,256,256]{2,1,0:T(8,128)(2,1)S(1)} copy-done((bf16[9,256,256]{2,1,0:T(8,128)(2,1)S(1)}, bf16[9,256,256]{2,1,0:T(8,128)(2,1)}, u32[]{:S(2)}) %copy-start) | copy-done | bytes 1179672
  1.9 0.0 copy-start.1
  1.9 1.1 %copy-done.1 = bf16[6,16,16,256]{3,2,1,0:T(8,128)(2,1)S(1)} copy-done((bf16[6,16,16,256]{3,2,1,0:T(8,128)(2,1)S(1)}, bf16[6,16,16,256]{3,2,1,0:T(8,128)(2,1)}, u32[]{:S(2)}) %copy-start.1) | copy-done | bytes 786456
  3.0 0.0 copy-start.2
  3.0 1.1 %copy-done.2 = bf16[6,16,16,256]{3,2,1,0:T(8,128)(2,1)S(1)} copy-done((bf16[6,16,16,256]{3,2,1,0:T(8,128)(2,1)S(1)}, bf16[6,16,16,256]{3,2,1,0:T(8,128)(2,1)}, u32[]{:S(2)}) %copy-start.2) | copy-done | bytes 786456
  4.2 0.0 copy-start.3
  4.2 0.7 %copy-done.3 = s32[6,8]{1,0:T(8,128)S(1)} copy-done((s32[6,8]{1,0:T(8,128)S(1)}, s32[6,8]{1,0:T(8,128)}, u32[]{:S(2)}) %copy-start.3) | copy-done | bytes 216
  4.9 0.0 copy-start.4
  4.9 0.7 %copy-done.4 = s32[6]{0:T(128)S(1)} copy-done((s32[6]{0:T(128)S(1)}, s32[6]{0:T(128)}, u32[]{:S(2)}) %copy-start.4) | copy-done | bytes 48
  5.5 42.0 %tile_conv_step.1 = (bf16[6,16,16,256]{3,2,1,0:T(8,128)(2,1)S(1)}, bf16[9,256,256]{2,1,0:T(8,128)(2,1)S(1)}, bf16[6,16,16,256]{3,2,1,0:T(8,128)(2,1)S(1)}) custom-call(bf16[6,16,16,256]{3,2,1,0:T(8,128)(2,1)S(1)} %copy-done.1, bf16[9,256,256]{2,1,0:T(8,128)(2,1)S(1)} %copy-done, bf16[6,16,16,256]{3,2,1,0:T(8,128)(2,1)S(1)} %copy-done.2, s32[6]{0:T(128)S(1)} %copy-done.4, ...), custom_call_target="tpu_custom_call" | custom-call | flops 5435817984 | bytes 8388608 | tf_op jit(solution)/shard_map/tile_conv_step/pallas_call | solution.py:364
  47.5 1.6 %convert_element_type.3 = f32[9,256,256]{2,1,0:T(8,128)} convert(bf16[9,256,256]{2,1,0:T(8,128)(2,1)S(1)} %get-tuple-element.7) | non-fusion elementwise | flops 589824 | bytes 3538944 | tf_op jit(solution)/shard_map/convert_element_type | solution.py:406
  49.2 0.9 %copy.10 = bf16[6,16,16,256]{3,2,1,0:T(8,128)(2,1)} copy(bf16[6,16,16,256]{3,2,1,0:T(8,128)(2,1)S(1)} %get-tuple-element.12) | data formatting | bytes 1572864
  50.0 0.9 %copy.11 = bf16[6,16,16,256]{3,2,1,0:T(8,128)(2,1)} copy(bf16[6,16,16,256]{3,2,1,0:T(8,128)(2,1)S(1)} %get-tuple-element.14) | data formatting | bytes 1572864
Async XLA Ops:
  0.6 1.3 %copy-start = (bf16[9,256,256]{2,1,0:T(8,128)(2,1)S(1)}, bf16[9,256,256]{2,1,0:T(8,128)(2,1)}, u32[]{:S(2)}) copy-start(bf16[9,256,256]{2,1,0:T(8,128)(2,1)} %weights.1) | copy-start | bytes 3538948
  1.9 1.1 %copy-start.1 = (bf16[6,16,16,256]{3,2,1,0:T(8,128)(2,1)S(1)}, bf16[6,16,16,256]{3,2,1,0:T(8,128)(2,1)}, u32[]{:S(2)}) copy-start(bf16[6,16,16,256]{3,2,1,0:T(8,128)(2,1)} %features.1) | copy-start | bytes 2359300
  3.0 1.1 %copy-start.2 = (bf16[6,16,16,256]{3,2,1,0:T(8,128)(2,1)S(1)}, bf16[6,16,16,256]{3,2,1,0:T(8,128)(2,1)}, u32[]{:S(2)}) copy-start(bf16[6,16,16,256]{3,2,1,0:T(8,128)(2,1)} %grad_out.1) | copy-start | bytes 2359300
  4.2 0.7 %copy-start.3 = (s32[6,8]{1,0:T(8,128)S(1)}, s32[6,8]{1,0:T(8,128)}, u32[]{:S(2)}) copy-start(s32[6,8]{1,0:T(8,128)} %links.1) | copy-start | bytes 580
  4.9 0.7 %copy-start.4 = (s32[6]{0:T(128)S(1)}, s32[6]{0:T(128)}, u32[]{:S(2)}) copy-start(s32[6]{0:T(128)} %tile_pos.1) | copy-start | bytes 76

commit v2 on v1

--- a/solution.py
+++ b/solution.py
@@ -26,14 +26,19 @@
 def kernel(
     count,
     scale,
+    features_hbm,
+    weights_hbm,
+    grad_out_hbm,
+    tile_pos_hbm,
+    links_hbm,
+    act,
+    total,
+    input_grad,
     features,
     weights,
     grad_out,
     tile_pos,
     links,
-    act,
-    grad_sum,
-    input_grad,
     ext_x,
     ext_g,
     above_x,
@@ -53,12 +58,12 @@
     fan_in,
     far_out,
     far_in,
-    total,
     halo_sems,
     core_sems,
     near_sems,
     fan_sems,
     far_sems,
+    load_sems,
 ):
     f32, bf16 = jnp.float32, jnp.bfloat16
     tiles, side, _, channels = features.shape
@@ -94,6 +99,17 @@
             device_id_type=MESH,
         )
 
+    pairs = (
+        (features_hbm, features),
+        (links_hbm, links),
+        (weights_hbm, weights),
+        (tile_pos_hbm, tile_pos),
+        (grad_out_hbm, grad_out),
+    )
+    loads = [pltpu.make_async_copy(*pair, load_sems.at[at]) for at, pair in enumerate(pairs)]
+    for load in loads:
+        load.start()
+
     has_prev, has_next = me > 0, me < count - 1
     barrier = pltpu.get_barrier_semaphore()
     peers = [core_peer, near_peer] + [fan_peer(step) for step in range(1, FAN)]
@@ -179,6 +195,9 @@
         border_rows(above, 0, tile, 0, 4, 5, 0, put)
         border_rows(below, side + 1, tile, 1, 6, 7, tiles, put)
 
+    loads[0].wait()
+    loads[1].wait()
+
     start_halo(0, features, above_x, below_x)
 
     def put_x(tile):
@@ -196,6 +215,9 @@
     @pl.loop(0, tiles)
     def _(tile):
         both_borders(above_x, below_x, tile, put_x(tile))
+
+    for load in loads[2:]:
+        load.wait()
 
     weight_mat_rows = taps * channels
 
@@ -320,7 +342,6 @@
                 fan_back(k, turn, fan).wait_send()
             near_back(k, near).wait_send()
             core_back(k, core).wait_send()
-            grad_sum[k] = total[k].reshape(channels, channels)
 
         @pl.when(step == taps)
         def _():
@@ -349,6 +370,23 @@
             input_grad[tile] = (back * gate).astype(bf16).reshape(side, side, channels)
 
 
+def finish(act_in, grad_in, back_in, act_out, grad_out, back_out, wide, sems):
+    taps = wide.shape[0]
+    copies = [
+        pltpu.make_async_copy(back_in, back_out, sems.at[0]),
+        pltpu.make_async_copy(act_in, act_out, sems.at[1]),
+    ]
+    for copy in copies:
+        copy.start()
+    for start in range(0, taps, taps // 3):
+        rows = pl.ds(start, taps // 3)
+        wide[rows] = grad_in[rows].astype(jnp.float32).reshape(wide[rows].shape)
+        copies.append(pltpu.make_async_copy(wide.at[rows], grad_out.at[rows], sems.at[len(copies)]))
+        copies[-1].start()
+    for copy in copies:
+        copy.wait()
+
+
 def body(count, features, weights, grad_out, tile_pos, neighbours):
     bf16, f32 = jnp.bfloat16, jnp.float32
     tiles, side, _, channels = features.shape
@@ -358,19 +396,24 @@
     far_rounds = int(math.log2(count // (4 * FAN)))
     table = pltpu.VMEM((2 * tiles + 1, side, channels), bf16)
     dma = pltpu.SemaphoreType.DMA
+    hbm = pl.BlockSpec(memory_space=pl.ANY)
     vmem = pl.BlockSpec(memory_space=pltpu.VMEM)
-    smem = pl.BlockSpec(memory_space=pltpu.SMEM)
     flops = 3 * 2 * tiles * side * side * taps * channels * channels
     act, grad_sum, input_grad = pl.pallas_call(
         functools.partial(kernel, count, scale),
         out_shape=(
-            jax.ShapeDtypeStruct(features.shape, bf16),
-            jax.ShapeDtypeStruct(weights.shape, bf16),
-            jax.ShapeDtypeStruct(features.shape, bf16),
+            pltpu.VMEM(features.shape, bf16),
+            pltpu.VMEM((taps,) + split, bf16),
+            pltpu.VMEM(features.shape, bf16),
         ),
-        in_specs=[vmem, vmem, vmem, smem, smem],
+        in_specs=[hbm] * 5,
         out_specs=(vmem, vmem, vmem),
         scratch_shapes=[
+            pltpu.VMEM(features.shape, bf16),
+            pltpu.VMEM(weights.shape, bf16),
+            pltpu.VMEM(features.shape, bf16),
+            pltpu.SMEM(tile_pos.shape, jnp.int32),
+            pltpu.SMEM(neighbours.shape, jnp.int32),
             pltpu.VMEM((3, tiles, side + 2, side, channels), bf16),
             pltpu.VMEM((3, side + 2, side, channels), bf16),
             table,
@@ -390,20 +433,35 @@
             pltpu.VMEM((taps, FAN - 1) + split[3:], bf16),
             pltpu.VMEM((taps, far_rounds) + split[3:], bf16),
             pltpu.VMEM((taps, far_rounds) + split[3:], bf16),
-            pltpu.VMEM((taps,) + split, bf16),
             dma((2, 2, 2)),
             dma((2, taps, 2)),
             dma((2, taps, 2)),
             dma((2, taps, FAN - 1, 2)),
             dma((taps, far_rounds, 2)),
+            dma((5,)),
         ],
         compiler_params=pltpu.CompilerParams(
-            collective_id=0, has_side_effects=True, vmem_limit_bytes=48 * 2**20
+            collective_id=0, has_side_effects=True, vmem_limit_bytes=60 * 2**20
         ),
         cost_estimate=pl.CostEstimate(flops=flops, bytes_accessed=2**23, transcendentals=0),
         name="tile_conv_step",
     )(features, weights, grad_out, tile_pos, neighbours)
-    return act, grad_sum.astype(f32), input_grad
+    return pl.pallas_call(
+        finish,
+        out_shape=(
+            jax.ShapeDtypeStruct(act.shape, bf16),
+            jax.ShapeDtypeStruct(weights.shape, f32),
+            jax.ShapeDtypeStruct(act.shape, bf16),
+        ),
+        in_specs=[vmem] * 3,
+        out_specs=(hbm, hbm, hbm),
+        scratch_shapes=[
+            pltpu.VMEM(weights.shape, f32),
+            dma((5,)),
+        ],
+        compiler_params=pltpu.CompilerParams(vmem_limit_bytes=8 * 2**20),
+        name="write_results",
+    )(act, grad_sum, input_grad)
 
 
 def solution(mesh):

time: 51.2 us -> 44.3 us (0.87)
  local copies, waits for them, and re-layouts: 6.63 us -> 0 us
  other arithmetic: 1.63 us -> 0 us
  Pallas kernels: 42 us -> 43.5 us
    unnamed x12 -> x0, local copies, waits for them, and re-layouts: 6.63 us -> none
    convert_element_type x1 -> x0, other arithmetic: 1.63 us -> none  [body(): return (act, grad_sum.astype(f32), input_grad)]
    pallas_call x1 -> x2, Pallas kernels: 42 us -> 43.5 us  [the longest x1 41.6 us: body(): pl.pallas_call(functools.partial(kernel, count, scale), out_shape=(pltpu....]
where the time goes in v2:
time: 44.3 us; the launch traced here: 44.2 us
  Pallas kernels  43.5 us (98%)
  between operations  0.64 us (1%)
    pallas_call x1, Pallas kernels, body(): pl.pallas_call(functools.partial(kernel, count, scale), out_shape=(pltpu....  41.6 us
    pallas_call x1, Pallas kernels, body(): pl.pallas_call(finish, out_shape=(jax.ShapeDtypeStruct(act.shape, bf16),...  1.96 us

profile of v2, /device:TPU:0, one launch (start us, length us, event | category | flops | bytes accessed | tf_op | source)
XLA Modules:
  0.0 44.2 jit_solution(17605885678731413900)
XLA Ops:
  0.6 41.6 %tile_conv_step.1 = (bf16[6,16,16,256]{3,2,1,0:T(8,128)(2,1)S(1)}, bf16[9,2,2,4,16,256]{5,4,3,2,1,0:T(8,128)(2,1)S(1)}, bf16[6,16,16,256]{3,2,1,0:T(8,128)(2,1)S(1)}) custom-call(bf16[6,16,16,256]{3,2,1,0:T(8,128)(2,1)} %features_hbm.1, bf16[9,256,256]{2,1,0:T(8,128)(2,1)} %weights_hbm.1, bf16[6,16,16,256]{3,2,1,0:T(8,128)(2,1)} %grad_out_hbm.1, ...), custom_call_target="tpu_custom_call" | custom-call | flops 5435817984 | bytes 8388608 | tf_op jit(solution)/shard_map/tile_conv_step/pallas_call | solution.py:402
  42.2 2.0 %write_results.1 = (bf16[6,16,16,256]{3,2,1,0:T(8,128)(2,1)}, f32[9,256,256]{2,1,0:T(8,128)}, bf16[6,16,16,256]{3,2,1,0:T(8,128)(2,1)}) custom-call(bf16[6,16,16,256]{3,2,1,0:T(8,128)(2,1)S(1)} %get-tuple-element.6.act_in, bf16[9,2,2,4,16,256]{5,4,3,2,1,0:T(8,128)(2,1)S(1)} %get-tuple-element.7.grad_in, bf16[6,16,16,256]{3,2,1,0:T(8,128)(2,1)S(1)} %get-tuple-element.8.back_in), custom_call_target="tpu_custom_call" | custom-call | tf_op jit(solution)/shard_map/write_results/pallas_call | solution.py:449

commit v3 on v2

--- a/solution.py
+++ b/solution.py
@@ -11,6 +11,7 @@
 ROOT_HALF = 0.7071067811865476
 INV_ROOT_TAU = 0.3989422804014327
 FAN = 4
+GROUP = 3
 LAG_CORE, LAG_NEAR, LAG_FAN, LAG_FAN_BACK, LAG_NEAR_BACK, LAG_CORE_BACK = (1, 3, 5, 7, 9, 10)
 MESH = pl.DeviceIdType.MESH
 
@@ -221,16 +222,17 @@
 
     weight_mat_rows = taps * channels
 
-    @pl.loop(0, tiles)
-    def _(tile):
+    def forward_dot(tile):
         pieces = [
             ext_x[b, tile, a : a + side].reshape(cells, channels) for a in range(3) for b in range(3)
         ]
-        preact = jnp.dot(
+        return jnp.dot(
             jnp.concatenate(pieces, axis=1),
             weights[...].reshape(weight_mat_rows, channels),
             preferred_element_type=f32,
         )
+
+    def forward_point(tile, preact):
         gate = jnp.where(tile_pos[tile] >= 0, 1.0, 0.0).astype(f32)
         cumulative = 0.5 * (1.0 + lax.erf(preact * ROOT_HALF))
         density = jnp.exp(-0.5 * preact * preact) * INV_ROOT_TAU
@@ -240,6 +242,15 @@
         pre_grad[tile] = slope.astype(bf16).reshape(side, side, channels)
         pre_grad_t[tile] = slope.T.astype(bf16)
 
+    batch = GROUP if tiles % GROUP == 0 else 1
+
+    @pl.loop(0, tiles // batch)
+    def _(turn):
+        group = [turn * batch + at for at in range(batch)]
+        preacts = [forward_dot(tile) for tile in group]
+        for tile, preact in zip(group, preacts):
+            forward_point(tile, preact)
+
     start_halo(1, pre_grad, above_g, below_g)
 
     def core_copy(k):
@@ -270,6 +281,12 @@
     def core_back(k, owner):
         block = total.at[k, owner]
         return send(block, block, core_sems.at[1, k], core_peer)
+
+    def put_g(tile):
+        def put(shift, rows, value):
+            ext_g[shift, tile, rows] = value
+
+        return put
 
     @pl.loop(0, taps + LAG_CORE_BACK)
     def _(step):
@@ -283,6 +300,8 @@
             core_out[k] = part[k, 1 - core].astype(bf16)
             core_copy(k).start()
             weights_t[k] = weights[k].astype(f32).T.astype(bf16)
+            own = jnp.minimum(k, tiles - 1)
+            inner_rows(pre_grad, own, put_g(own))
 
         @pl.when((step >= LAG_CORE) & (step < taps + LAG_CORE))
         def _():
@@ -343,21 +362,19 @@
             near_back(k, near).wait_send()
             core_back(k, core).wait_send()
 
-        @pl.when(step == taps)
+        @pl.when(step == taps - 1)
         def _():
             wait_halo(1, above_g, below_g)
 
+            @pl.loop(0, tiles)
+            def _(tile):
+                both_borders(above_g, below_g, tile, put_g(tile))
+
         @pl.when((step >= taps) & (step < taps + tiles))
         def _():
             tile = step - taps
-
-            def put(shift, rows, value):
-                ext_g[shift, rows] = value
-
-            inner_rows(pre_grad, tile, put)
-            both_borders(above_g, below_g, tile, put)
             pieces = [
-                ext_g[2 - b, 2 - a : 2 - a + side].reshape(cells, channels)
+                ext_g[2 - b, tile, 2 - a : 2 - a + side].reshape(cells, channels)
                 for a in range(3)
                 for b in range(3)
             ]
@@ -415,7 +432,7 @@
             pltpu.SMEM(tile_pos.shape, jnp.int32),
             pltpu.SMEM(neighbours.shape, jnp.int32),
             pltpu.VMEM((3, tiles, side + 2, side, channels), bf16),
-            pltpu.VMEM((3, side + 2, side, channels), bf16),
+            pltpu.VMEM((3, tiles, side + 2, side, channels), bf16),
             table,
             table,
             table,

time: 44.3 us -> 43.1 us (0.973)
  Pallas kernels: 43.5 us -> 42.4 us
    pallas_call x1, Pallas kernels: 41.6 us -> 40.4 us  [body(): pl.pallas_call(functools.partial(kernel, count, scale), out_shape=(pltpu....]
where the time goes in v3:
time: 43.1 us; the launch traced here: 43 us
  Pallas kernels  42.4 us (98%)
  between operations  0.64 us (1%)
    pallas_call x1, Pallas kernels, body(): pl.pallas_call(functools.partial(kernel, count, scale), out_shape=(pltpu....  40.4 us
    pallas_call x1, Pallas kernels, body(): pl.pallas_call(finish, out_shape=(jax.ShapeDtypeStruct(act.shape, bf16),...  1.96 us

profile of v3, /device:TPU:0, one launch (start us, length us, event | category | flops | bytes accessed | tf_op | source)
XLA Modules:
  0.0 43.0 jit_solution(2420601093603266329)
XLA Ops:
  0.6 40.4 %tile_conv_step.1 = (bf16[6,16,16,256]{3,2,1,0:T(8,128)(2,1)S(1)}, bf16[9,2,2,4,16,256]{5,4,3,2,1,0:T(8,128)(2,1)S(1)}, bf16[6,16,16,256]{3,2,1,0:T(8,128)(2,1)S(1)}) custom-call(bf16[6,16,16,256]{3,2,1,0:T(8,128)(2,1)} %features_hbm.1, bf16[9,256,256]{2,1,0:T(8,128)(2,1)} %weights_hbm.1, bf16[6,16,16,256]{3,2,1,0:T(8,128)(2,1)} %grad_out_hbm.1, ...), custom_call_target="tpu_custom_call" | custom-call | flops 5435817984 | bytes 8388608 | tf_op jit(solution)/shard_map/tile_conv_step/pallas_call | solution.py:419
  41.0 2.0 %write_results.1 = (bf16[6,16,16,256]{3,2,1,0:T(8,128)(2,1)}, f32[9,256,256]{2,1,0:T(8,128)}, bf16[6,16,16,256]{3,2,1,0:T(8,128)(2,1)}) custom-call(bf16[6,16,16,256]{3,2,1,0:T(8,128)(2,1)S(1)} %get-tuple-element.6.act_in, bf16[9,2,2,4,16,256]{5,4,3,2,1,0:T(8,128)(2,1)S(1)} %get-tuple-element.7.grad_in, bf16[6,16,16,256]{3,2,1,0:T(8,128)(2,1)S(1)} %get-tuple-element.8.back_in), custom_call_target="tpu_custom_call" | custom-call | tf_op jit(solution)/shard_map/write_results/pallas_call | solution.py:466
